TPU v7x, 32 devices: a whole 2x2x4 slice. The times are simulated.
32 devices in a mesh: groups: 2 (over y), latent: 4 (over z), width: 4 (over x, core).
Axes of the slice: x: 2, y: 2, z: 4, core: 2. Of those that a mesh axis runs over, the one named last changes fastest.
Arguments:
- acts: bfloat16 [512, 5120], P(('groups', 'latent'), 'width'), parts along dimension 0, may hold values from -6 to 6
- dec_bias: float32 [10240], P(('groups', 'width')), parts along dimension 0, may hold values from -3 to 3
- enc_weight: bfloat16 [5120, 1024], P('width', ('groups', 'latent')), parts along dimension 1, may hold values from -0.078125 to 0.078125
- enc_bias: float32 [1024], P(('groups', 'latent')), parts along dimension 0, may hold values from -3 to 3
- dec_weight: bfloat16 [1024, 5120], P(('groups', 'latent'), 'width'), parts along dimension 0, may hold values from -0.25 to 0.25
- enc_m: float32 [5120, 1024], P('width', ('groups', 'latent')), parts along dimension 1, may hold values from -0.6 to 0.6
- enc_v: float32 [5120, 1024], P('width', ('groups', 'latent')), parts along dimension 1, may hold values from 0.0001 to 0.01
- dec_m: float32 [1024, 5120], P(('groups', 'latent'), 'width'), parts along dimension 0, may hold values from -0.6 to 0.6
- dec_v: float32 [1024, 5120], P(('groups', 'latent'), 'width'), parts along dimension 0, may hold values from 0.0001 to 0.01
- bias_m: float32 [1024], P(('groups', 'latent')), parts along dimension 0, may hold values from -0.6 to 0.6
- bias_v: float32 [1024], P(('groups', 'latent')), parts along dimension 0, may hold values from 0.0001 to 0.01
Outputs:
- enc_moment: float32 [5120, 1024], P('width', ('groups', 'latent')), parts along dimension 1
- enc_second: float32 [5120, 1024], P('width', ('groups', 'latent')), parts along dimension 1
- enc_step: bfloat16 [5120, 1024], P('width', ('groups', 'latent')), parts along dimension 1
- dec_moment: float32 [1024, 5120], P(('groups', 'latent'), 'width'), parts along dimension 0
- dec_second: float32 [1024, 5120], P(('groups', 'latent'), 'width'), parts along dimension 0
- dec_step: bfloat16 [1024, 5120], P(('groups', 'latent'), 'width'), parts along dimension 0
- bias_moment: float32 [1024], P(('groups', 'latent')), parts along dimension 0
- bias_second: float32 [1024], P(('groups', 'latent')), parts along dimension 0
- bias_step: bfloat16 [1024], P(('groups', 'latent')), parts along dimension 0
There are 2 independent parts, one for each index of `groups`. A program takes and returns all parts, laid end to end along the dimension named above; each array names one. Nothing has to cross between parts.
All inputs are finite; a program needn't handle non-finite values.
Results may differ from a plain program's by a relative error of at most 0.006.
The roundings to bfloat16 on the way count: a program that leaves them out, or rounds other values in their place, can miss the bound.
Values may be sent and summed in bfloat16 or wider, within the bound.
A program may use at most 64 MiB of HBM per device.

v0:
```python
import jax
import jax.numpy as jnp
from jax import lax
from jax.sharding import PartitionSpec as P

ADAM_STEP = 10


BETA_ONE = 0.9
BETA_TWO = 0.95
EPSILON = 1e-08
SPARSITY = 0.5
SHARPNESS = 4.0


def adam_update(moment, second, grad):
    moment_new = BETA_ONE * moment + (1.0 - BETA_ONE) * grad
    second_new = BETA_TWO * second + (1.0 - BETA_TWO) * grad * grad
    update_step = (
        moment_new
        / (1.0 - BETA_ONE**ADAM_STEP)
        / (jnp.sqrt(second_new / (1.0 - BETA_TWO**ADAM_STEP)) + EPSILON)
    )
    return (moment_new, second_new, update_step.astype(jnp.bfloat16))


def inner_rows(left, right):
    return lax.dot_general(
        left, right, (((0,), (0,)), ((), ())), preferred_element_type=jnp.float32
    )


def inner_cols(left, right):
    return lax.dot_general(
        left, right, (((1,), (1,)), ((), ())), preferred_element_type=jnp.float32
    )


def local(
    acts, dec_bias, enc_weight, enc_bias, dec_weight, enc_m, enc_v, dec_m, dec_v, bias_m, bias_v
):
    lat_groups = lax.axis_size("latent")
    rows_local = acts.shape[0]
    rows_all = rows_local * lat_groups
    incoming = lax.all_gather(acts, "latent", axis=0, tiled=True)
    centered_block = (incoming.astype(jnp.float32) - dec_bias).astype(jnp.bfloat16)
    product = jnp.dot(centered_block, enc_weight, preferred_element_type=jnp.float32)
    pre_part = product
    raw_rows = incoming
    centered = centered_block
    pre_part, raw_rows, centered = (pre_part, raw_rows, centered)
    pre = lax.psum(pre_part, "width") + enc_bias
    latent_code = (jax.nn.softplus(SHARPNESS * pre) / SHARPNESS).astype(jnp.bfloat16)
    codes = latent_code
    rebuilt = (
        lax.psum_scatter(
            jnp.dot(codes, dec_weight, preferred_element_type=jnp.float32),
            "latent",
            scatter_dimension=0,
            tiled=True,
        )
        + dec_bias
    )
    grad_out = (2.0 / rows_all * (rebuilt - acts.astype(jnp.float32))).astype(jnp.bfloat16)
    incoming = lax.all_gather(grad_out, "latent", axis=0, tiled=True)
    codes = latent_code
    dec_grad = inner_rows(codes, incoming)
    code_part = inner_cols(incoming, dec_weight)
    dec_grad, code_part = (dec_grad, code_part)
    code_grad = lax.psum(code_part, "width") + SPARSITY / rows_all
    pre_grad = (code_grad * jax.nn.sigmoid(SHARPNESS * pre)).astype(jnp.bfloat16)
    enc_grad = inner_rows(centered, pre_grad)
    bias_grad = jnp.sum(pre_grad.astype(jnp.float32), axis=0)
    enc_moment, enc_second, enc_step = adam_update(enc_m, enc_v, enc_grad)
    dec_moment, dec_second, dec_step = adam_update(dec_m, dec_v, dec_grad)
    bias_moment, bias_second, bias_step = adam_update(bias_m, bias_v, bias_grad)
    return (
        enc_moment,
        enc_second,
        enc_step,
        dec_moment,
        dec_second,
        dec_step,
        bias_moment,
        bias_second,
        bias_step,
    )


def solution(mesh):
    in_specs = (
        P(("groups", "latent"), "width"),
        P(("groups", "width")),
        P("width", ("groups", "latent")),
        P(("groups", "latent")),
        P(("groups", "latent"), "width"),
        P("width", ("groups", "latent")),
        P("width", ("groups", "latent")),
        P(("groups", "latent"), "width"),
        P(("groups", "latent"), "width"),
        P(("groups", "latent")),
        P(("groups", "latent")),
    )
    out_specs = (
        P("width", ("groups", "latent")),
        P("width", ("groups", "latent")),
        P("width", ("groups", "latent")),
        P(("groups", "latent"), "width"),
        P(("groups", "latent"), "width"),
        P(("groups", "latent"), "width"),
        P(("groups", "latent")),
        P(("groups", "latent")),
        P(("groups", "latent")),
    )
    return jax.shard_map(local, mesh=mesh, in_specs=in_specs, out_specs=out_specs, check_vma=False)
```

profile of v0, /device:TPU:0, one launch (start us, length us, event | category | flops | bytes accessed | tf_op | source)
XLA Modules:
  0.0 155.3 jit_solution(8856377542071319319)
XLA Ops:
  7.2 0.0 copy-start
  7.2 0.0 all-reduce.3.cloned.1.call-start
  7.2 20.0 %all_gather.6 = bf16[256,1280]{1,0:T(8,128)(2,1)S(1)} all-gather(bf16[64,1280]{1,0:T(8,128)(2,1)} %param.11), channel_id=1, replica_groups=mesh['groups'=2,'latent'=4,'width'=4] {'latent'}, dimensions={0}, use_global_device_ids=true | all-gather | bytes 819200 | tf_op jit(solution)/shard_map/all_gather | solution.py:45
  27.2 2.0 %fusion.3 = f32[256,128]{1,0:T(8,128)} fusion(bf16[1280,128]{1,0:T(8,128)(2,1)} %param.13, bf16[256,1280]{1,0:T(8,128)(2,1)S(1)} %all_gather.6, f32[1280]{0:T(1024)} %param.12), kind=kOutput, calls=%fused_computation.10 | convolution fusion | flops 84869120 | bytes 1119232 | tf_op jit(solution)/shard_map/dot_general | solution.py:47
  29.2 0.0 all-reduce.3.cloned.1.call-update
  29.2 0.0 copy-start.3
  29.2 0.0 reduce-scatter.2.cloned.1.call-start
  29.3 31.8 %all-reduce.3.cloned.1.call-done = f32[256,128]{1,0:T(8,128)} async-done(((f32[256,128]{1,0:T(8,128)}), f32[256,128]{1,0:T(8,128)}) %all-reduce.3.cloned.1.call-update) | async-done | bytes 131088 | tf_op jit(solution)/shard_map/psum | solution.py:52
  61.1 2.4 %fusion.10 = f32[256,1280]{1,0:T(8,128)} fusion(bf16[128,1280]{1,0:T(8,128)(2,1)S(1)} %copy-done, f32[256,128]{1,0:T(8,128)} %all-reduce.3.cloned.1.call-done, f32[128]{0:T(128)S(1)} %copy-done.4), kind=kOutput, calls=%fused_computation.24 | convolution fusion | flops 84213760 | bytes 1769984 | tf_op jit(solution)/shard_map/dot_general | solution.py:57
  63.4 0.0 reduce-scatter.2.cloned.1.call-update
  63.5 0.0 copy-start.7
  63.5 0.0 copy-start.8
  63.5 0.0 all-reduce.5.cloned.1.call-start
  63.5 31.3 %reduce-scatter.2.cloned.1.call-done = f32[64,1280]{1,0:T(8,128)} async-done(((f32[256,1280]{1,0:T(8,128)}), f32[64,1280]{1,0:T(8,128)}) %reduce-scatter.2.cloned.1.call-update) | async-done | bytes 327696 | tf_op jit(solution)/shard_map/reduce_scatter | solution.py:56
  94.8 1.0 multiply_convert_fusion
  95.8 16.9 %all_gather.7 = bf16[256,1280]{1,0:T(8,128)(2,1)S(1)} all-gather(bf16[64,1280]{1,0:T(8,128)(2,1)S(1)} %multiply_convert_fusion), channel_id=1, replica_groups=mesh['groups'=2,'latent'=4,'width'=4] {'latent'}, dimensions={0}, use_global_device_ids=true | all-gather | bytes 819200 | tf_op jit(solution)/shard_map/all_gather | solution.py:65
  112.7 1.0 fusion.15
  113.7 0.0 all-reduce.5.cloned.1.call-update
  113.7 0.0 copy-start.5
  113.8 1.8 %divide_convert_fusion = (bf16[128,1280]{1,0:T(8,128)(2,1)}, f32[128,1280]{1,0:T(8,128)}, f32[128,1280]{1,0:T(8,128)}) fusion(f32[128,1280]{1,0:T(8,128)S(1)} %copy-done.7, f32[128,1280]{1,0:T(8,128)S(1)} %copy-done.8, bf16[256,1280]{1,0:T(8,128)(2,1)S(1)} %all_gather.7, f32[256,128]{1,0:T(8,128)S(1)} %copy-done.2, f32[128]{0:T(128)S(1)} %copy-done.4), kind=kOutput, calls=%fused_computation.5 | convolution fusion | flops 86179840 | bytes 3736064 | tf_op jit(solution)/shard_map/dot_general | solution.py:28
  115.6 28.5 %all-reduce.5.cloned.1.call-done = f32[256,128]{1,0:T(8,128)} async-done(((f32[256,128]{1,0:T(8,128)}), f32[256,128]{1,0:T(8,128)}) %all-reduce.5.cloned.1.call-update) | async-done | bytes 131088 | tf_op jit(solution)/shard_map/psum | solution.py:70
  144.1 1.0 convert_reduce_fusion
  145.1 0.5 fusion.7
  145.7 3.1 %divide_convert_fusion.1 = (bf16[1280,128]{1,0:T(8,128)(2,1)}, f32[1280,128]{1,0:T(8,128)}, f32[1280,128]{1,0:T(8,128)}) fusion(f32[1280,128]{1,0:T(8,128)} %param.17, f32[1280,128]{1,0:T(8,128)} %param.16, bf16[256,128]{1,0:T(8,128)(2,1)S(1)} %get-tuple-element.13, bf16[256,1280]{1,0:T(8,128)(2,1)S(1)} %all_gather.6, f32[1280]{0:T(1024)S(1)} %copy-done.3), kind=kOutput, calls=%fused_computation.7 | convolution fusion | flops 86835200 | bytes 3675136 | tf_op jit(solution)/shard_map/dot_general | solution.py:28
  (13 shorter events, 0.0 us)
Async XLA Ops:
  7.2 53.9 %copy-start = (bf16[128,1280]{1,0:T(8,128)(2,1)S(1)}, bf16[128,1280]{1,0:T(8,128)(2,1)}, u32[]{:S(2)}) copy-start(bf16[128,1280]{1,0:T(8,128)(2,1)} %param.15) | copy-start | bytes 983044
  7.2 53.9 %copy-start.4 = (f32[128]{0:T(128)S(1)}, f32[128]{0:T(128)}, u32[]{:S(2)}) copy-start(f32[128]{0:T(128)} %param.14) | copy-start | bytes 1540
  7.2 53.8 %all-reduce.3.cloned.1.call-start = ((), (), s32[]{:S(2)}) async-start(), calls=%async_computation.1 | async-start | bytes 262144 | tf_op jit(solution)/shard_map/psum | solution.py:52
  29.2 65.6 %copy-start.1 = (bf16[64,1280]{1,0:T(8,128)(2,1)S(1)}, bf16[64,1280]{1,0:T(8,128)(2,1)}, u32[]{:S(2)}) copy-start(bf16[64,1280]{1,0:T(8,128)(2,1)} %param.11) | copy-start | bytes 491524
  29.2 65.6 %copy-start.3 = (f32[1280]{0:T(1024)S(1)}, f32[1280]{0:T(1024)}, u32[]{:S(2)}) copy-start(f32[1280]{0:T(1024)} %param.12) | copy-start | bytes 15364
  29.2 65.6 %reduce-scatter.2.cloned.1.call-start = ((), (), s32[]{:S(2)}) async-start(), calls=%async_computation.2 | async-start | bytes 1638400 | tf_op jit(solution)/shard_map/reduce_scatter | solution.py:56
  63.4 50.3 %copy-start.2 = (f32[256,128]{1,0:T(8,128)S(1)}, f32[256,128]{1,0:T(8,128)}, u32[]{:S(2)}) copy-start(f32[256,128]{1,0:T(8,128)} %all-reduce.3.cloned.1.call-done) | copy-start | bytes 393220
  63.5 50.3 %copy-start.7 = (f32[128,1280]{1,0:T(8,128)S(1)}, f32[128,1280]{1,0:T(8,128)}, u32[]{:S(2)}) copy-start(f32[128,1280]{1,0:T(8,128)} %param.19) | copy-start | bytes 1966084
  63.5 50.3 %copy-start.8 = (f32[128,1280]{1,0:T(8,128)S(1)}, f32[128,1280]{1,0:T(8,128)}, u32[]{:S(2)}) copy-start(f32[128,1280]{1,0:T(8,128)} %param.18) | copy-start | bytes 1966084
  63.5 80.7 %all-reduce.5.cloned.1.call-start = ((), (), s32[]{:S(2)}) async-start(), calls=%async_computation.3 | async-start | bytes 262144 | tf_op jit(solution)/shard_map/psum | solution.py:70
  113.7 31.4 %copy-start.5 = (f32[128]{0:T(128)S(1)}, f32[128]{0:T(128)}, u32[]{:S(2)}) copy-start(f32[128]{0:T(128)} %param.21) | copy-start | bytes 1540
  113.8 31.4 %copy-start.6 = (f32[128]{0:T(128)S(1)}, f32[128]{0:T(128)}, u32[]{:S(2)}) copy-start(f32[128]{0:T(128)} %param.20) | copy-start | bytes 1540
Sparse Core Ops, SparseCore 0:
  29.3 31.6 all-reduce.2
  63.6 31.1 reduce-scatter.1
  113.8 30.2 all-reduce.4
where the time goes:
time: 156 us; the launch traced here: 155 us
  waiting for transfers between devices  91.6 us (59%)
  blocking collectives  36.8 us (24%)
  between operations  13.9 us (9%)
  matrix products  10.3 us (7%)
  other arithmetic  2.54 us (2%)
    psum x1, waiting for transfers between devices, local(): pre = lax.psum(pre_part, 'width') + enc_bias  31.8 us
    reduce_scatter x1, waiting for transfers between devices, local(): lax.psum_scatter(jnp.dot(codes, dec_weight, preferred_element_type=jnp.fl...  31.3 us
    psum x1, waiting for transfers between devices, local(): code_grad = lax.psum(code_part, 'width') + SPARSITY / rows_all  28.5 us
    all_gather x1, blocking collectives, local(): incoming = lax.all_gather(acts, 'latent', axis=0, tiled=True)  20 us
    all_gather x1, blocking collectives, local(): incoming = lax.all_gather(grad_out, 'latent', axis=0, tiled=True)  16.9 us
    dot_general x2, matrix products, inner_rows(): lax.dot_general(left, right, (((0,), (0,)), ((), ())), preferred_element_...  4.93 us
  transfers between devices with their start and end apart: 3, of which 3 were waited for; matrix products, arithmetic and copies ran while one was open for 1% of the time, Pallas kernels for 0%

commit v1 on v0

--- a/solution.py
+++ b/solution.py
@@ -1,6 +1,10 @@
+import functools
+
 import jax
 import jax.numpy as jnp
 from jax import lax
+from jax.experimental import pallas as pl
+from jax.experimental.pallas import tpu as pltpu
 from jax.sharding import PartitionSpec as P
 
 ADAM_STEP = 10
@@ -11,6 +15,8 @@
 EPSILON = 1e-08
 SPARSITY = 0.5
 SHARPNESS = 4.0
+
+MESH = pl.DeviceIdType.MESH
 
 
 def adam_update(moment, second, grad):
@@ -36,7 +42,7 @@
     )
 
 
-def local(
+def local_large(
     acts, dec_bias, enc_weight, enc_bias, dec_weight, enc_m, enc_v, dec_m, dec_v, bias_m, bias_v
 ):
     lat_groups = lax.axis_size("latent")
@@ -87,6 +93,339 @@
     )
 
 
+def exchange_kernel(
+    n,
+    nw,
+    acts_ref,
+    dec_bias_ref,
+    enc_weight_ref,
+    enc_bias_ref,
+    dec_weight_ref,
+    centered,
+    codes,
+    grad_out,
+    pre_grad,
+    acts_all,
+    pre_parts,
+    code_parts,
+    slope,
+    product,
+    total,
+    left_sum,
+    right_sum,
+    to_right,
+    to_left,
+    acts_recv,
+    acts_send_right,
+    acts_send_left,
+    left_recv,
+    right_recv,
+    right_send,
+    left_send,
+    pre_recv,
+    pre_send,
+    code_recv,
+    code_send,
+):
+    place = lax.axis_index("latent")
+    mine = lax.axis_index("width")
+    rows_all = n * acts_ref.shape[0]
+    peers = [lax.rem(mine + k, nw) for k in range(1, nw)]
+
+    barrier = pltpu.get_barrier_semaphore()
+    for peer in peers:
+        pl.semaphore_signal(barrier, inc=1, device_id={"width": peer}, device_id_type=MESH)
+
+    @pl.when(place > 0)
+    def _():
+        pl.semaphore_signal(barrier, inc=1, device_id={"latent": place - 1}, device_id_type=MESH)
+
+    @pl.when(place < n - 1)
+    def _():
+        pl.semaphore_signal(barrier, inc=1, device_id={"latent": place + 1}, device_id_type=MESH)
+
+    pl.semaphore_wait(
+        barrier, nw - 1 + jnp.where(place > 0, 1, 0) + jnp.where(place < n - 1, 1, 0)
+    )
+
+    def program(z):
+        sent = []
+        right = {"latent": place + 1}
+        left = {"latent": place - 1}
+        some = right if z < n - 1 else left
+
+        def acts_block(b):
+            return acts_ref if b == z else acts_all.at[b]
+
+        def copy(src, dst, send, recv, where):
+            return pltpu.make_async_remote_copy(
+                src_ref=src,
+                dst_ref=dst,
+                send_sem=send,
+                recv_sem=recv,
+                device_id=where,
+                device_id_type=MESH,
+            )
+
+        def send(*arguments):
+            descriptor = copy(*arguments)
+            descriptor.start()
+            sent.append(descriptor)
+
+        def acts_right(b):
+            send(acts_block(b), acts_all.at[b], acts_send_right.at[b], acts_recv.at[b], right)
+
+        def acts_left(b):
+            send(acts_block(b), acts_all.at[b], acts_send_left.at[b], acts_recv.at[b], left)
+
+        def to_peers(parts, b, send_sem, recv_sem):
+            for k in range(1, nw):
+                block = parts.at[mine, b]
+                send(block, block, send_sem.at[k, b], recv_sem.at[k, b], {"width": peers[k - 1]})
+
+        def from_peers(parts, b, send_sem, recv_sem):
+            for k in range(1, nw):
+                block = parts.at[mine, b]
+                copy(
+                    block, block, send_sem.at[k, b], recv_sem.at[k, b], {"width": peers[k - 1]}
+                ).wait_recv()
+            total = parts[0, b]
+            for other in range(1, nw):
+                total = total + parts[other, b]
+            return total
+
+        def start_pre(b):
+            rounded = (acts_block(b)[...].astype(jnp.float32) - dec_bias_ref[...]).astype(
+                jnp.bfloat16
+            )
+            centered[b] = rounded
+            pre_parts[mine, b] = jnp.dot(
+                rounded, enc_weight_ref[...], preferred_element_type=jnp.float32
+            )
+            to_peers(pre_parts, b, pre_send, pre_recv)
+
+        def finish_pre(b):
+            scaled = SHARPNESS * (from_peers(pre_parts, b, pre_send, pre_recv) + enc_bias_ref[...])
+            small = jnp.exp(-jnp.abs(scaled))
+            code = ((jnp.maximum(scaled, 0.0) + jnp.log1p(small)) / SHARPNESS).astype(jnp.bfloat16)
+            slope[b] = jnp.where(scaled >= 0, 1.0, small) / (1.0 + small)
+            codes[b] = code
+            own = jnp.dot(code, dec_weight_ref[...], preferred_element_type=jnp.float32)
+            product[b] = own
+            total[b] = own + dec_bias_ref[...]
+
+        def sum_right(i):
+            partial = product[i]
+            if z > 0:
+                arrived = left_sum[i]
+                partial = partial + arrived
+                total[i] = total[i] + arrived
+            if z < n - 1:
+                to_right[i] = partial
+                send(to_right.at[i], left_sum.at[i], right_send.at[i], left_recv.at[i], right)
+
+        def sum_left(i):
+            partial = product[i]
+            if z < n - 1:
+                arrived = right_sum[i]
+                partial = partial + arrived
+                total[i] = total[i] + arrived
+            if z > 0:
+                to_left[i] = partial
+                send(to_left.at[i], right_sum.at[i], left_send.at[i], right_recv.at[i], left)
+
+        def start_code(i):
+            rounded = (2.0 / rows_all * (total[i] - acts_block(i)[...].astype(jnp.float32))).astype(
+                jnp.bfloat16
+            )
+            grad_out[i] = rounded
+            code_parts[mine, i] = inner_cols(rounded, dec_weight_ref[...])
+            to_peers(code_parts, i, code_send, code_recv)
+
+        def finish_code(i):
+            code_grad = from_peers(code_parts, i, code_send, code_recv) + SPARSITY / rows_all
+            pre_grad[i] = (code_grad * slope[i]).astype(jnp.bfloat16)
+
+        if z < n - 1:
+            acts_right(z)
+        if z > 0:
+            acts_left(z)
+        start_pre(z)
+        waiting_pre, waiting_code = [z], []
+        for step in range(1, 2 * n):
+            for b in waiting_pre:
+                finish_pre(b)
+                if z == 0:
+                    sum_right(b)
+                if z == n - 1:
+                    sum_left(b)
+            for i in waiting_code:
+                finish_code(i)
+            waiting_pre, waiting_code = [], []
+            for b, onward in ((z - step, acts_right), (z + step, acts_left)):
+                if 0 <= b < n:
+                    copy(
+                        acts_all.at[b],
+                        acts_all.at[b],
+                        acts_send_right.at[b],
+                        acts_recv.at[b],
+                        some,
+                    ).wait_recv()
+                    if (onward is acts_right and z < n - 1) or (onward is acts_left and z > 0):
+                        onward(b)
+                    waiting_pre.append(b)
+            for b in waiting_pre:
+                start_pre(b)
+            i = step - 1 - z
+            if z > 0 and 0 <= i < n:
+                copy(
+                    to_right.at[i], left_sum.at[i], right_send.at[i], left_recv.at[i], some
+                ).wait_recv()
+                sum_right(i)
+            i = 2 * n - 1 - z - step
+            if z < n - 1 and 0 <= i < n:
+                copy(
+                    to_left.at[i], right_sum.at[i], left_send.at[i], right_recv.at[i], some
+                ).wait_recv()
+                sum_left(i)
+            for i in range(n):
+                from_left = z + 1 + i if z > 0 else 0
+                from_right = 2 * n - 1 - z - i if z < n - 1 else 0
+                if max(from_left, from_right) == step:
+                    start_code(i)
+                    waiting_code.append(i)
+        for i in waiting_code:
+            finish_code(i)
+        for descriptor in sent:
+            descriptor.wait_send()
+
+    for z in range(n):
+        pl.when(place == z)(functools.partial(program, z))
+
+
+def exchange(n, nw, acts, dec_bias, enc_weight, enc_bias, dec_weight):
+    rows, width = acts.shape
+    latents = enc_weight.shape[1]
+    wide = (n, rows, width)
+    narrow = (n, rows, latents)
+    parts = (nw,) + narrow
+    dma = pltpu.SemaphoreType.DMA
+    vmem = pl.BlockSpec(memory_space=pltpu.VMEM)
+    return pl.pallas_call(
+        functools.partial(exchange_kernel, n, nw),
+        out_shape=[
+            jax.ShapeDtypeStruct(wide, jnp.bfloat16),
+            jax.ShapeDtypeStruct(narrow, jnp.bfloat16),
+            jax.ShapeDtypeStruct(wide, jnp.bfloat16),
+            jax.ShapeDtypeStruct(narrow, jnp.bfloat16),
+        ],
+        in_specs=[vmem] * 5,
+        out_specs=[vmem] * 4,
+        scratch_shapes=[
+            pltpu.VMEM(wide, jnp.bfloat16),
+            pltpu.VMEM(parts, jnp.float32),
+            pltpu.VMEM(parts, jnp.float32),
+            pltpu.VMEM(narrow, jnp.float32),
+            pltpu.VMEM(wide, jnp.float32),
+            pltpu.VMEM(wide, jnp.float32),
+            pltpu.VMEM(wide, jnp.float32),
+            pltpu.VMEM(wide, jnp.float32),
+            pltpu.VMEM(wide, jnp.float32),
+            pltpu.VMEM(wide, jnp.float32),
+        ]
+        + [dma((n,))] * 7
+        + [dma((nw, n))] * 4,
+        compiler_params=pltpu.CompilerParams(
+            collective_id=0, has_side_effects=True, vmem_limit_bytes=32 * 2**20
+        ),
+        name="exchange",
+    )(acts, dec_bias[None, :], enc_weight, enc_bias[None, :], dec_weight)
+
+
+def update_kernel(
+    centered,
+    codes,
+    grad_out,
+    pre_grad,
+    enc_m,
+    enc_v,
+    dec_m,
+    dec_v,
+    bias_m,
+    bias_v,
+    enc_moment,
+    enc_second,
+    enc_step,
+    dec_moment,
+    dec_second,
+    dec_step,
+    bias_moment,
+    bias_second,
+    bias_step,
+):
+    dec_grad = inner_rows(codes[...], grad_out[...])
+    dec_moment[...], dec_second[...], dec_step[...] = adam_update(dec_m[...], dec_v[...], dec_grad)
+    enc_grad = inner_rows(centered[...], pre_grad[...])
+    enc_moment[...], enc_second[...], enc_step[...] = adam_update(enc_m[...], enc_v[...], enc_grad)
+
+    @pl.when(pl.program_id(0) == 0)
+    def _():
+        bias_grad = jnp.sum(pre_grad[...].astype(jnp.float32), axis=0, keepdims=True)
+        bias_moment[...], bias_second[...], bias_step[...] = adam_update(
+            bias_m[...], bias_v[...], bias_grad
+        )
+
+
+def update(centered, codes, grad_out, pre_grad, enc_m, enc_v, dec_m, dec_v, bias_m, bias_v):
+    rows, width = centered.shape
+    latents = codes.shape[1]
+    tile = 256 if width % 256 == 0 else width
+    slab = pl.BlockSpec((rows, tile), lambda j: (0, j))
+    whole = pl.BlockSpec((rows, latents), lambda j: (0, 0))
+    enc = pl.BlockSpec((tile, latents), lambda j: (j, 0))
+    dec = pl.BlockSpec((latents, tile), lambda j: (0, j))
+    bias = pl.BlockSpec((1, latents), lambda j: (0, 0))
+
+    def like(shape, dtype):
+        return jax.ShapeDtypeStruct(shape, dtype)
+
+    kinds = (jnp.float32, jnp.float32, jnp.bfloat16)
+    return pl.pallas_call(
+        update_kernel,
+        grid=(width // tile,),
+        out_shape=[like((width, latents), kind) for kind in kinds]
+        + [like((latents, width), kind) for kind in kinds]
+        + [like((1, latents), kind) for kind in kinds],
+        in_specs=[slab, whole, slab, whole, enc, enc, dec, dec, bias, bias],
+        out_specs=[enc] * 3 + [dec] * 3 + [bias] * 3,
+        compiler_params=pltpu.CompilerParams(vmem_limit_bytes=32 * 2**20),
+        name="update",
+    )(centered, codes, grad_out, pre_grad, enc_m, enc_v, dec_m, dec_v, bias_m, bias_v)
+
+
+def local_small(
+    acts, dec_bias, enc_weight, enc_bias, dec_weight, enc_m, enc_v, dec_m, dec_v, bias_m, bias_v
+):
+    n, nw = lax.axis_size("latent"), lax.axis_size("width")
+    width, latents = acts.shape[1], enc_weight.shape[1]
+    centered, codes, grad_out, pre_grad = exchange(
+        n, nw, acts, dec_bias, enc_weight, enc_bias, dec_weight
+    )
+    results = update(
+        centered.reshape(-1, width),
+        codes.reshape(-1, latents),
+        grad_out.reshape(-1, width),
+        pre_grad.reshape(-1, latents),
+        enc_m,
+        enc_v,
+        dec_m,
+        dec_v,
+        bias_m[None, :],
+        bias_v[None, :],
+    )
+    return (*results[:6], *(one.reshape(-1) for one in results[6:]))
+
+
 def solution(mesh):
     in_specs = (
         P(("groups", "latent"), "width"),
@@ -112,4 +451,5 @@
         P(("groups", "latent")),
         P(("groups", "latent")),
     )
+    local = local_small if mesh.shape["latent"] <= 4 else local_large
     return jax.shard_map(local, mesh=mesh, in_specs=in_specs, out_specs=out_specs, check_vma=False)

time: 156 us -> 72.9 us (0.47)
  waiting for transfers between devices: 91.6 us -> 0 us
  Pallas kernels: 0 us -> 63.6 us
  blocking collectives: 36.8 us -> 0 us
  between operations: 13.9 us -> 0.69 us
  matrix products: 10.3 us -> 0 us
  local copies, waits for them, and re-layouts: 0.06 us -> 8.19 us
  other arithmetic: 2.54 us -> 0 us
    pallas_call x0 -> x2, Pallas kernels: none -> 63.6 us  [the longest x1 59.8 us: exchange(): pl.pallas_call(functools.partial(exchange_kernel, n, nw), out_shape=[jax....]
    psum x2 -> x0, waiting for transfers between devices: 60.3 us -> none  [the longest x1 31.8 us: local(): pre = lax.psum(pre_part, 'width') + enc_bias]
    all_gather x2 -> x0, blocking collectives: 36.8 us -> none  [the longest x1 20 us: local(): incoming = lax.all_gather(acts, 'latent', axis=0, tiled=True)]
    reduce_scatter x1 -> x0, waiting for transfers between devices: 31.3 us -> none  [local(): lax.psum_scatter(jnp.dot(codes, dec_weight, preferred_element_type=jnp.fl...]
    dot_general x5 -> x0, matrix products: 10.3 us -> none  [the longest x2 4.93 us: inner_rows(): lax.dot_general(left, right, (((0,), (0,)), ((), ())), preferred_element_...]
    unnamed x18 -> x20, local copies, waits for them, and re-layouts: 0.06 us -> 7.43 us
    convert_element_type x2 -> x0, other arithmetic: 1.57 us -> none  [the longest x1 1.03 us: local(): (2.0 / rows_all * (rebuilt - acts.astype(jnp.float32))).astype(jnp.bfloat16)]
  transfers between devices with their start and end apart: 3 -> 0, of which waited for: 3 -> 0; matrix products, arithmetic and copies ran while one was open for 1% -> 0% of each run, Pallas kernels for 0% -> 0%
where the time goes in v1:
time: 72.9 us; the launch traced here: 72.5 us
  Pallas kernels  63.6 us (87%)
  local copies, waits for them, and re-layouts  8.19 us (11%)
    pallas_call x1, Pallas kernels, exchange(): pl.pallas_call(functools.partial(exchange_kernel, n, nw), out_shape=[jax....  59.8 us
    unnamed x20, local copies, waits for them, and re-layouts  7.43 us
    pallas_call x1, Pallas kernels, update(): pl.pallas_call(update_kernel, grid=(width // tile,), out_shape=[like((wid...  3.86 us

profile of v1, /device:TPU:0, one launch (start us, length us, event | category | flops | bytes accessed | tf_op | source)
XLA Modules:
  0.0 72.5 jit_solution(5512719214313467376)
XLA Ops:
  0.6 0.0 copy-start
  0.7 0.8 %broadcast_in_dim.12.dec_bias_ref = f32[1,1280]{1,0:T(1,128)S(1)} reshape(f32[1280]{0:T(1024)} %param.12) | data formatting | bytes 10240 | tf_op jit(solution)/shard_map/broadcast_in_dim | solution.py:342
  1.4 0.0 copy-start.4
  1.4 1.0 %copy-done.4 = bf16[1280,128]{1,0:T(8,128)(2,1)S(1)} copy-done((bf16[1280,128]{1,0:T(8,128)(2,1)S(1)}, bf16[1280,128]{1,0:T(8,128)(2,1)}, u32[]{:S(2)}) %copy-start.4) | copy-done | bytes 327704
  2.4 0.0 copy-start.5
  2.4 1.0 %copy-done.5 = bf16[128,1280]{1,0:T(8,128)(2,1)S(1)} copy-done((bf16[128,1280]{1,0:T(8,128)(2,1)S(1)}, bf16[128,1280]{1,0:T(8,128)(2,1)}, u32[]{:S(2)}) %copy-start.5) | copy-done | bytes 327704
  3.4 0.0 copy-start.6
  3.4 0.9 %copy-done.6 = bf16[64,1280]{1,0:T(8,128)(2,1)S(1)} copy-done((bf16[64,1280]{1,0:T(8,128)(2,1)S(1)}, bf16[64,1280]{1,0:T(8,128)(2,1)}, u32[]{:S(2)}) %copy-start.6) | copy-done | bytes 163864
  4.3 0.0 copy-start.9
  4.3 0.7 copy-done.9
  4.9 59.8 %exchange.1 = (bf16[4,64,1280]{2,1,0:T(8,128)(2,1)S(1)}, bf16[4,64,128]{2,1,0:T(8,128)(2,1)S(1)}, bf16[4,64,1280]{2,1,0:T(8,128)(2,1)S(1)}, bf16[4,64,128]{2,1,0:T(8,128)(2,1)S(1)}) custom-call(bf16[64,1280]{1,0:T(8,128)(2,1)S(1)} %copy-done.6, f32[1,1280]{1,0:T(1,128)S(1)} %broadcast_in_dim.12.dec_bias_ref, bf16[1280,128]{1,0:T(8,128)(2,1)S(1)} %copy-done.4, ...), custom_call_target="tpu_custom_call" | custom-call | tf_op jit(solution)/shard_map/exchange/pallas_call | solution.py:314
  64.7 0.0 copy-start.7
  64.7 0.0 copy-start.8
  64.7 0.0 copy-done
  64.7 0.6 copy-done.7
  65.4 0.0 copy-done.8
  65.4 0.0 copy-start.1
  65.4 1.1 %copy-done.1 = f32[1280,128]{1,0:T(8,128)S(1)} copy-done((f32[1280,128]{1,0:T(8,128)S(1)}, f32[1280,128]{1,0:T(8,128)}, u32[]{:S(2)}) %copy-start.1) | copy-done | bytes 655384
  66.5 0.0 copy-start.2
  66.5 1.1 %copy-done.2 = f32[128,1280]{1,0:T(8,128)S(1)} copy-done((f32[128,1280]{1,0:T(8,128)S(1)}, f32[128,1280]{1,0:T(8,128)}, u32[]{:S(2)}) %copy-start.2) | copy-done | bytes 655384
  67.6 0.0 copy-start.3
  67.6 1.1 %copy-done.3 = f32[128,1280]{1,0:T(8,128)S(1)} copy-done((f32[128,1280]{1,0:T(8,128)S(1)}, f32[128,1280]{1,0:T(8,128)}, u32[]{:S(2)}) %copy-start.3) | copy-done | bytes 655384
  68.6 3.9 %update.1 = (f32[1280,128]{1,0:T(8,128)}, f32[1280,128]{1,0:T(8,128)}, bf16[1280,128]{1,0:T(8,128)(2,1)}, f32[128,1280]{1,0:T(8,128)}, f32[128,1280]{1,0:T(8,128...) custom-call(bf16[256,1280]{1,0:T(8,128)(2,1)S(1)} %bitcast.10, ...), custom_call_target="tpu_custom_call" | custom-call | tf_op jit(solution)/shard_map/update/pallas_call | solution.py:393
Async XLA Ops:
  0.6 64.1 %copy-start = (f32[1280,128]{1,0:T(8,128)S(1)}, f32[1280,128]{1,0:T(8,128)}, u32[]{:S(2)}) copy-start(f32[1280,128]{1,0:T(8,128)} %enc_m.1) | copy-start | bytes 1966084
  1.4 1.0 %copy-start.4 = (bf16[1280,128]{1,0:T(8,128)(2,1)S(1)}, bf16[1280,128]{1,0:T(8,128)(2,1)}, u32[]{:S(2)}) copy-start(bf16[1280,128]{1,0:T(8,128)(2,1)} %enc_weight_ref.1) | copy-start | bytes 983044
  2.4 1.0 %copy-start.5 = (bf16[128,1280]{1,0:T(8,128)(2,1)S(1)}, bf16[128,1280]{1,0:T(8,128)(2,1)}, u32[]{:S(2)}) copy-start(bf16[128,1280]{1,0:T(8,128)(2,1)} %dec_weight_ref.1) | copy-start | bytes 983044
  3.4 0.9 %copy-start.6 = (bf16[64,1280]{1,0:T(8,128)(2,1)S(1)}, bf16[64,1280]{1,0:T(8,128)(2,1)}, u32[]{:S(2)}) copy-start(bf16[64,1280]{1,0:T(8,128)(2,1)} %acts_ref.1) | copy-start | bytes 491524
  4.3 0.7 copy-start.9
  64.7 0.7 copy-start.7
  64.7 0.7 copy-start.8
  65.4 1.1 %copy-start.1 = (f32[1280,128]{1,0:T(8,128)S(1)}, f32[1280,128]{1,0:T(8,128)}, u32[]{:S(2)}) copy-start(f32[1280,128]{1,0:T(8,128)} %enc_v.1) | copy-start | bytes 1966084
  66.5 1.1 %copy-start.2 = (f32[128,1280]{1,0:T(8,128)S(1)}, f32[128,1280]{1,0:T(8,128)}, u32[]{:S(2)}) copy-start(f32[128,1280]{1,0:T(8,128)} %dec_m.1) | copy-start | bytes 1966084
  67.6 1.1 %copy-start.3 = (f32[128,1280]{1,0:T(8,128)S(1)}, f32[128,1280]{1,0:T(8,128)}, u32[]{:S(2)}) copy-start(f32[128,1280]{1,0:T(8,128)} %dec_v.1) | copy-start | bytes 1966084

commit v2 on v1

--- a/solution.py
+++ b/solution.py
@@ -109,19 +109,17 @@
     pre_parts,
     code_parts,
     slope,
-    product,
-    total,
-    left_sum,
-    right_sum,
-    to_right,
-    to_left,
+    dec_all,
+    codes_all,
     acts_recv,
     acts_send_right,
     acts_send_left,
-    left_recv,
-    right_recv,
-    right_send,
-    left_send,
+    dec_recv,
+    dec_send,
+    codes_recv,
+    codes_send,
+    grad_recv,
+    grad_send,
     pre_recv,
     pre_send,
     code_recv,
@@ -130,6 +128,7 @@
     place = lax.axis_index("latent")
     mine = lax.axis_index("width")
     rows_all = n * acts_ref.shape[0]
+    half = acts_ref.shape[1] // 2
     peers = [lax.rem(mine + k, nw) for k in range(1, nw)]
 
     barrier = pltpu.get_barrier_semaphore()
@@ -152,7 +151,11 @@
         sent = []
         right = {"latent": place + 1}
         left = {"latent": place - 1}
-        some = right if z < n - 1 else left
+        inward = right if z < n // 2 else left
+        outward = left if z < n // 2 else right
+
+        def columns(h):
+            return pl.ds(h * half, half)
 
         def acts_block(b):
             return acts_ref if b == z else acts_all.at[b]
@@ -210,92 +213,128 @@
             code = ((jnp.maximum(scaled, 0.0) + jnp.log1p(small)) / SHARPNESS).astype(jnp.bfloat16)
             slope[b] = jnp.where(scaled >= 0, 1.0, small) / (1.0 + small)
             codes[b] = code
-            own = jnp.dot(code, dec_weight_ref[...], preferred_element_type=jnp.float32)
-            product[b] = own
-            total[b] = own + dec_bias_ref[...]
-
-        def sum_right(i):
-            partial = product[i]
-            if z > 0:
-                arrived = left_sum[i]
-                partial = partial + arrived
-                total[i] = total[i] + arrived
-            if z < n - 1:
-                to_right[i] = partial
-                send(to_right.at[i], left_sum.at[i], right_send.at[i], left_recv.at[i], right)
-
-        def sum_left(i):
-            partial = product[i]
-            if z < n - 1:
-                arrived = right_sum[i]
-                partial = partial + arrived
-                total[i] = total[i] + arrived
-            if z > 0:
-                to_left[i] = partial
-                send(to_left.at[i], right_sum.at[i], left_send.at[i], right_recv.at[i], left)
+            send_codes(z, b)
+
+        def codes_block(k, b):
+            return codes.at[b] if k == z else codes_all.at[k, b]
+
+        def send_codes(k, b):
+            send(
+                codes_block(k, b),
+                codes_all.at[k, b],
+                codes_send.at[k, b],
+                codes_recv.at[k, b],
+                inward,
+            )
+
+        def wait_codes(k, b):
+            block = codes_all.at[k, b]
+            copy(block, block, codes_send.at[k, b], codes_recv.at[k, b], inward).wait_recv()
+
+        def dec_block(k, h):
+            return dec_weight_ref.at[:, columns(h)] if k == z else dec_all.at[k, h]
+
+        def send_dec(k, h):
+            send(
+                dec_block(k, h), dec_all.at[k, h], dec_send.at[k, h], dec_recv.at[k, h], inward
+            )
+
+        def wait_dec(k, h):
+            block = dec_all.at[k, h]
+            copy(block, block, dec_send.at[k, h], dec_recv.at[k, h], inward).wait_recv()
+
+        def make_grad(h, i):
+            rebuilt = dec_bias_ref[:, columns(h)]
+            for k in range(n):
+                rebuilt = rebuilt + jnp.dot(
+                    codes_block(k, i)[...],
+                    dec_block(k, h)[...],
+                    preferred_element_type=jnp.float32,
+                )
+            raw = acts_block(i)[:, columns(h)].astype(jnp.float32)
+            grad_out[i, :, columns(h)] = (2.0 / rows_all * (rebuilt - raw)).astype(jnp.bfloat16)
+            block = grad_out.at[i, :, columns(h)]
+            send(block, block, grad_send.at[h, i], grad_recv.at[h, i], outward)
+
+        def wait_grad(h, i):
+            block = grad_out.at[i, :, columns(h)]
+            copy(block, block, grad_send.at[h, i], grad_recv.at[h, i], inward).wait_recv()
 
         def start_code(i):
-            rounded = (2.0 / rows_all * (total[i] - acts_block(i)[...].astype(jnp.float32))).astype(
-                jnp.bfloat16
-            )
-            grad_out[i] = rounded
-            code_parts[mine, i] = inner_cols(rounded, dec_weight_ref[...])
+            code_parts[mine, i] = inner_cols(grad_out[i], dec_weight_ref[...])
             to_peers(code_parts, i, code_send, code_recv)
 
         def finish_code(i):
             code_grad = from_peers(code_parts, i, code_send, code_recv) + SPARSITY / rows_all
             pre_grad[i] = (code_grad * slope[i]).astype(jnp.bfloat16)
 
-        if z < n - 1:
-            acts_right(z)
-        if z > 0:
-            acts_left(z)
-        start_pre(z)
-        waiting_pre, waiting_code = [z], []
-        for step in range(1, 2 * n):
-            for b in waiting_pre:
-                finish_pre(b)
-                if z == 0:
-                    sum_right(b)
-                if z == n - 1:
-                    sum_left(b)
-            for i in waiting_code:
+        def wait_acts(b):
+            block = acts_all.at[b]
+            copy(block, block, acts_send_right.at[b], acts_recv.at[b], inward).wait_recv()
+
+        if z in (0, 3):
+            order = [0, 1, 2, 3] if z == 0 else [3, 2, 1, 0]
+            (acts_right if z == 0 else acts_left)(z)
+            start_pre(z)
+            send_dec(z, 0)
+            send_dec(z, 1)
+            for before, b in zip(order, order[1:]):
+                finish_pre(before)
+                wait_acts(b)
+                start_pre(b)
+            finish_pre(order[3])
+            for i in range(n):
+                wait_grad(0, i)
+            for i in range(n):
+                wait_grad(1, i)
+                start_code(i)
+                if i > 0:
+                    finish_code(i - 1)
+            finish_code(n - 1)
+        else:
+            end, middle, far = (0, 2, 3) if z == 1 else (3, 1, 0)
+            to_end, to_middle = (acts_left, acts_right) if z == 1 else (acts_right, acts_left)
+            to_middle(z)
+            to_end(z)
+            start_pre(z)
+            finish_pre(z)
+            wait_acts(end)
+            to_middle(end)
+            wait_acts(middle)
+            to_end(middle)
+            start_pre(end)
+            start_pre(middle)
+            send_dec(z, 0)
+            finish_pre(end)
+            finish_pre(middle)
+            wait_dec(end, 0)
+            send_dec(end, 0)
+            wait_acts(far)
+            to_end(far)
+            start_pre(far)
+            send_dec(z, 1)
+            for b in (end, z):
+                wait_codes(end, b)
+                send_codes(end, b)
+            finish_pre(far)
+            wait_dec(end, 1)
+            send_dec(end, 1)
+            for b in (middle, far):
+                wait_codes(end, b)
+                send_codes(end, b)
+            for k in (middle, far):
+                for b in range(n):
+                    wait_codes(k, b)
+                wait_dec(k, 0)
+            for i in range(n):
+                make_grad(0, i)
+            for k in (middle, far):
+                wait_dec(k, 1)
+            for i in range(n):
+                make_grad(1, i)
+                start_code(i)
+            for i in range(n):
                 finish_code(i)
-            waiting_pre, waiting_code = [], []
-            for b, onward in ((z - step, acts_right), (z + step, acts_left)):
-                if 0 <= b < n:
-                    copy(
-                        acts_all.at[b],
-                        acts_all.at[b],
-                        acts_send_right.at[b],
-                        acts_recv.at[b],
-                        some,
-                    ).wait_recv()
-                    if (onward is acts_right and z < n - 1) or (onward is acts_left and z > 0):
-                        onward(b)
-                    waiting_pre.append(b)
-            for b in waiting_pre:
-                start_pre(b)
-            i = step - 1 - z
-            if z > 0 and 0 <= i < n:
-                copy(
-                    to_right.at[i], left_sum.at[i], right_send.at[i], left_recv.at[i], some
-                ).wait_recv()
-                sum_right(i)
-            i = 2 * n - 1 - z - step
-            if z < n - 1 and 0 <= i < n:
-                copy(
-                    to_left.at[i], right_sum.at[i], left_send.at[i], right_recv.at[i], some
-                ).wait_recv()
-                sum_left(i)
-            for i in range(n):
-                from_left = z + 1 + i if z > 0 else 0
-                from_right = 2 * n - 1 - z - i if z < n - 1 else 0
-                if max(from_left, from_right) == step:
-                    start_code(i)
-                    waiting_code.append(i)
-        for i in waiting_code:
-            finish_code(i)
         for descriptor in sent:
             descriptor.wait_send()
 
@@ -326,17 +365,21 @@
             pltpu.VMEM(parts, jnp.float32),
             pltpu.VMEM(parts, jnp.float32),
             pltpu.VMEM(narrow, jnp.float32),
-            pltpu.VMEM(wide, jnp.float32),
-            pltpu.VMEM(wide, jnp.float32),
-            pltpu.VMEM(wide, jnp.float32),
-            pltpu.VMEM(wide, jnp.float32),
-            pltpu.VMEM(wide, jnp.float32),
-            pltpu.VMEM(wide, jnp.float32),
+            pltpu.VMEM((n, 2, latents, width // 2), jnp.bfloat16),
+            pltpu.VMEM((n, n, rows, latents), jnp.bfloat16),
+            dma((n,)),
+            dma((n,)),
+            dma((n,)),
+            dma((n, 2)),
+            dma((n, 2)),
+            dma((n, n)),
+            dma((n, n)),
+            dma((2, n)),
+            dma((2, n)),
         ]
-        + [dma((n,))] * 7
         + [dma((nw, n))] * 4,
         compiler_params=pltpu.CompilerParams(
-            collective_id=0, has_side_effects=True, vmem_limit_bytes=32 * 2**20
+            collective_id=0, has_side_effects=True, vmem_limit_bytes=56 * 2**20
         ),
         name="exchange",
     )(acts, dec_bias[None, :], enc_weight, enc_bias[None, :], dec_weight)
@@ -398,7 +441,7 @@
         + [like((1, latents), kind) for kind in kinds],
         in_specs=[slab, whole, slab, whole, enc, enc, dec, dec, bias, bias],
         out_specs=[enc] * 3 + [dec] * 3 + [bias] * 3,
-        compiler_params=pltpu.CompilerParams(vmem_limit_bytes=32 * 2**20),
+        compiler_params=pltpu.CompilerParams(vmem_limit_bytes=56 * 2**20),
         name="update",
     )(centered, codes, grad_out, pre_grad, enc_m, enc_v, dec_m, dec_v, bias_m, bias_v)
 
@@ -451,5 +494,5 @@
         P(("groups", "latent")),
         P(("groups", "latent")),
     )
-    local = local_small if mesh.shape["latent"] <= 4 else local_large
+    local = local_small if mesh.shape["latent"] == 4 else local_large
     return jax.shard_map(local, mesh=mesh, in_specs=in_specs, out_specs=out_specs, check_vma=False)

time: 72.9 us -> 63.9 us (0.88)
  local copies, waits for them, and re-layouts: 8.19 us -> 1.29 us
  Pallas kernels: 63.6 us -> 61.7 us
    unnamed x20 -> x0, local copies, waits for them, and re-layouts: 7.43 us -> none
    pallas_call x1, Pallas kernels: 59.8 us -> 54.9 us  [exchange(): pl.pallas_call(functools.partial(exchange_kernel, n, nw), out_shape=[jax....]
    pallas_call x1, Pallas kernels: 3.86 us -> 6.74 us  [update(): pl.pallas_call(update_kernel, grid=(width // tile,), out_shape=[like((wid...]
where the time goes in v2:
time: 63.9 us; the launch traced here: 63.6 us
  Pallas kernels  61.7 us (97%)
  local copies, waits for them, and re-layouts  1.29 us (2%)
  between operations  0.65 us (1%)
    pallas_call x1, Pallas kernels, exchange(): pl.pallas_call(functools.partial(exchange_kernel, n, nw), out_shape=[jax....  54.9 us
    pallas_call x1, Pallas kernels, update(): pl.pallas_call(update_kernel, grid=(width // tile,), out_shape=[like((wid...  6.74 us
    broadcast_in_dim x1, local copies, waits for them, and re-layouts, exchange(): dec_bias[None, :]  1.29 us

profile of v2, /device:TPU:0, one launch (start us, length us, event | category | flops | bytes accessed | tf_op | source)
XLA Modules:
  0.0 63.6 jit_solution(8309745905140365836)
XLA Ops:
  0.6 1.3 %broadcast_in_dim.12.dec_bias_ref = f32[1,1280]{1,0:T(1,128)} reshape(f32[1280]{0:T(1024)} %param.12) | data formatting | bytes 10240 | tf_op jit(solution)/shard_map/broadcast_in_dim | solution.py:385
  1.9 54.9 %exchange.1 = (bf16[4,64,1280]{2,1,0:T(8,128)(2,1)}, bf16[4,64,128]{2,1,0:T(8,128)(2,1)}, bf16[4,64,1280]{2,1,0:T(8,128)(2,1)}, bf16[4,64,128]{2,1,0:T(8,128)(2,1)}) custom-call(bf16[64,1280]{1,0:T(8,128)(2,1)} %acts_ref.1, f32[1,1280]{1,0:T(1,128)} %broadcast_in_dim.12.dec_bias_ref, bf16[1280,128]{1,0:T(8,128)(2,1)} %enc_weight_ref.1, f32[1,128]{1,0:T(1,128)} %bitcast.16, ...), custom_call_target="tpu_custom_call" | custom-call | tf_op jit(solution)/shard_map/exchange/pallas_call | solution.py:353
  56.9 6.7 %update.1 = (f32[1280,128]{1,0:T(8,128)}, f32[1280,128]{1,0:T(8,128)}, bf16[1280,128]{1,0:T(8,128)(2,1)}, f32[128,1280]{1,0:T(8,128)}, f32[128,1280]{1,0:T(8,128...) custom-call(bf16[256,1280]{1,0:T(8,128)(2,1)} %bitcast.10, ...), custom_call_target="tpu_custom_call" | custom-call | tf_op jit(solution)/shard_map/update/pallas_call | solution.py:436
